TPU v7x, 32 devices: a whole 2x2x4 slice. The times are simulated.
32 devices in a mesh: groups: 2 (over x), wide: 16 (over z, y, core).
Axes of the slice: x: 2, y: 2, z: 4, core: 2. Of those that a mesh axis runs over, the one named last changes fastest.
Arguments:
- sources: bfloat16 [64, 65536], P('groups', 'wide'), parts along dimension 0, may hold values from -6 to 6
- near_blocks: bfloat16 [3072, 256, 256], P(('groups', 'wide')), parts along dimension 0, may hold values from -0.375 to 0.375
- scale_table: float32 [1536], P('groups'), parts along dimension 0, may hold values from 0.25 to 1
- scale_index: int32 [3072], P(('groups', 'wide')), parts along dimension 0, may hold values from 0 to 767
- near_source: int32 [3072], P(('groups', 'wide')), parts along dimension 0, may hold values from 0 to 15
- near_target: int32 [3072], P(('groups', 'wide')), parts along dimension 0, may hold values from 0 to 255, as said below
- basis_in: bfloat16 [512, 64, 256], P(('groups', 'wide')), parts along dimension 0, may hold values from -0.375 to 0.375
- basis_out: bfloat16 [512, 64, 256], P(('groups', 'wide')), parts along dimension 0, may hold values from -0.1875 to 0.1875
- couplings: bfloat16 [8192, 64, 64], P(('groups', 'wide')), parts along dimension 0, may hold values from -0.75 to 0.75
- far_source: int32 [8192], P(('groups', 'wide')), parts along dimension 0, may hold values from 0 to 255
- far_target: int32 [8192], P(('groups', 'wide')), parts along dimension 0, may hold values from 0 to 15
Outputs:
- potentials: bfloat16 [64, 65536], P('groups', 'wide'), parts along dimension 0
There are 2 independent parts, one for each index of `groups`. A program takes and returns all parts, laid end to end along the dimension named above; each array names one. Nothing has to cross between parts.
Inputs may be any that keep to these rules, and one draw needn't show every extreme that they name: `near_target`: in each aligned block of 96 entries (the pairs of one device), at most 6 entries name clusters of one owner (owner = cluster // 16), and some owner is named exactly 6 times in every block.
All inputs are finite; a program needn't handle non-finite values.
Results may differ from a plain program's by a relative error of at most 0.0054.
Values may be sent and summed in bfloat16 or wider, within the bound.
A program may use at most 128 MiB of HBM per device.

v0:
```python
import jax
import jax.numpy as jnp
from jax import lax
from jax.sharding import PartitionSpec as P


def shards(
    sources,
    near_blocks,
    scale_table,
    scale_index,
    near_source,
    near_target,
    basis_in,
    basis_out,
    couplings,
    far_source,
    far_target,
):
    owners = lax.axis_size("wide")
    clusters_here = basis_in.shape[0]
    rank_width = basis_in.shape[1]
    block = basis_in.shape[2]
    rhs_count = sources.shape[0]
    far_count = couplings.shape[0]
    local_x = sources.reshape(rhs_count, clusters_here, block)
    picked = jnp.take(local_x, near_source, axis=1)
    table_pos = jnp.arange(scale_table.shape[0], dtype=jnp.int32)
    factor = jnp.sum(
        jnp.where(scale_index[:, None] == table_pos[None, :], scale_table[None, :], 0.0), axis=1
    )
    products = (
        jnp.einsum("rps,pts->prt", picked, near_blocks, preferred_element_type=jnp.float32)
        * factor[:, None, None]
    )
    local_sums = (
        jnp.zeros((owners * clusters_here, rhs_count, block), jnp.float32)
        .at[near_target]
        .add(products)
    )
    outgoing = local_sums.astype(jnp.bfloat16)
    arrived = lax.all_to_all(outgoing, "wide", split_axis=0, concat_axis=0, tiled=True)
    near_part = jnp.sum(
        arrived.reshape(owners, clusters_here, rhs_count, block).astype(jnp.float32), axis=0
    )
    skeleton = jnp.einsum(
        "rcs,cks->crk", local_x, basis_in, preferred_element_type=jnp.float32
    ).astype(jnp.bfloat16)
    skeleton = skeleton.reshape(clusters_here, rhs_count * rank_width)
    every = lax.all_gather(skeleton, "wide", axis=0, tiled=True)
    chosen = jnp.take(every, far_source, axis=0).reshape(far_count, rhs_count, rank_width)
    coupled = jnp.einsum("frk,fkm->frm", chosen, couplings, preferred_element_type=jnp.float32)
    cluster_ids = jnp.arange(clusters_here, dtype=jnp.int32)
    member_far = (far_target[None, :] == cluster_ids[:, None]).astype(jnp.float32)
    combined = jnp.einsum(
        "cf,frm->crm", member_far, coupled, precision=lax.Precision.HIGHEST
    ).astype(jnp.bfloat16)
    far_part = jnp.einsum("crk,cks->crs", combined, basis_out, preferred_element_type=jnp.float32)
    total = (near_part + far_part).astype(jnp.bfloat16)
    return jnp.transpose(total, (1, 0, 2)).reshape(rhs_count, clusters_here * block)


def solution(mesh):
    in_specs = (
        P("groups", "wide"),
        P(("groups", "wide"), None, None),
        P("groups"),
        P(("groups", "wide")),
        P(("groups", "wide")),
        P(("groups", "wide")),
        P(("groups", "wide"), None, None),
        P(("groups", "wide"), None, None),
        P(("groups", "wide"), None, None),
        P(("groups", "wide")),
        P(("groups", "wide")),
    )
    out_specs = P("groups", "wide")
    return jax.shard_map(shards, mesh=mesh, in_specs=in_specs, out_specs=out_specs, check_vma=False)
```

profile of v0, /device:TPU:15, one launch (start us, length us, event | category | flops | bytes accessed | tf_op | source)
XLA Modules:
  0.0 163.6 jit_solution(7975557914081540699)
XLA Ops:
  6.5 0.0 copy-start
  6.5 0.7 compare_select_fusion.1
  7.3 0.7 compare_and_fusion.1
  7.9 1.0 copy.41
  8.9 0.7 compare_select_fusion.2
  9.6 0.7 gather_fusion
  10.3 0.9 select_reduce_fusion
  11.2 10.1 %convolution_multiply_fusion = f32[96,32,256]{2,1,0:T(8,128)} fusion(bf16[96,256,256]{2,1,0:T(8,128)(2,1)} %param.12, bf16[96,32,256]{2,1,0:T(8,128)(2,1)S(1)} %gather_fusion, f32[96]{0:T(128)S(1)} %select_reduce_fusion, pred[96]{0:T(512)(128)(4,1)S(1)} %compare_and_fusion.1), kind=kOutput, calls=%fused_computation.6 | convolution fusion | flops 404226048 | bytes 17301984 | tf_op jit(solution)/shard_map/rps,pts->prt/dot_general | solution.py:33
  21.3 4.3 %broadcast_in_dim.48 = f32[256,32,256]{2,1,0:T(8,128)} broadcast(f32[]{:T(128)} %constant.18.clone.1), dimensions={} | broadcast | bytes 8388612 | tf_op jit(solution)/shard_map/broadcast_in_dim | solution.py:37
  25.6 15.4 %scatter_fusion = f32[256,32,256]{2,1,0:T(8,128)} fusion(f32[256,32,256]{2,1,0:T(8,128)} %broadcast_in_dim.48, s32[96]{0:T(128)S(1)} %compare_select_fusion.2, f32[96,32,256]{2,1,0:T(8,128)} %convolution_multiply_fusion), kind=kCustom, calls=%fused_computation.2 | custom fusion | flops 786432 | bytes 9437568 | tf_op jit(solution)/shard_map/scatter-add | solution.py:39
  41.0 6.0 %convert_element_type.23 = bf16[256,32,256]{2,1,0:T(8,128)(2,1)} convert(f32[256,32,256]{2,1,0:T(8,128)} %scatter_fusion) | non-fusion elementwise | flops 2097152 | bytes 12582912 | tf_op jit(solution)/shard_map/convert_element_type | solution.py:41
  47.0 0.0 copy-start.2
  47.0 0.0 copy-start.3
  47.0 0.0 copy-start.1
  47.0 6.9 %all-to-all-start = ((bf16[256,32,256]{2,1,0:T(8,128)(2,1)}), bf16[256,32,256]{2,1,0:T(8,128)(2,1)}, u32[]{:S(2)}, u32[]{:S(2)}) async-start(bf16[256,32,256]{2,1,0:T(8,128)(2,1)} %convert_element_type.23), calls=%async_computation | async-start | bytes 8388608 | tf_op jit(solution)/shard_map/all_to_all | solution.py:42
  53.9 0.0 copy-start.5
  53.9 0.2 all-gather.2.cloned.1.call-start
  54.1 0.0 copy-done.2
  54.1 0.0 copy-done.3
  54.1 0.3 convolution_convert_fusion
  54.4 0.8 reshape.34
  55.2 0.0 all-gather.2.cloned.1.call-update
  55.3 0.0 copy-done.1
  55.3 6.7 %copy.27 = bf16[256,64,64]{2,1,0:T(8,128)(2,1)} copy(bf16[256,64,64]{0,2,1:T(8,128)(2,1)S(1)} %copy-done.1) | data formatting | bytes 4194304 | tf_op args[8]
  61.9 0.0 copy-done.5
  62.0 69.7 %all-gather.2.cloned.1.call-done = bf16[256,2048]{1,0:T(8,128)(2,1)} async-done(((bf16[16,2048]{1,0:T(8,128)(2,1)}), bf16[256,2048]{1,0:T(8,128)(2,1)}) %all-gather.2.cloned.1.call-update) | async-done | bytes 1048592 | tf_op jit(solution)/shard_map/all_gather | solution.py:50
  131.7 3.7 %gather_fusion.1 = bf16[256,2048]{1,0:T(8,128)(2,1)S(1)} fusion(bf16[256,2048]{1,0:T(8,128)(2,1)} %all-gather.2.cloned.1.call-done, s32[1024]{0:T(1024)S(1)} %pad_clamp_fusion), kind=kCustom, calls=%fused_computation.1 | custom fusion | bytes 2098176 | tf_op jit(solution)/shard_map/jit(_take)/gather | solution.py:51
  135.4 0.5 copy.25
  135.9 1.1 broadcast_select_fusion
  137.1 3.9 %copy.26 = bf16[256,32,64]{2,1,0:T(8,128)(2,1)S(1)} copy(bf16[256,32,64]{0,2,1:T(8,128)(2,1)} %broadcast_select_fusion) | data formatting | bytes 2097152 | tf_op jit(solution)/shard_map/jit(_take)/select_n | solution.py:51
  141.0 0.0 copy-start.4
  141.0 3.4 %fusion.16 = f32[256,32,64]{2,1,0:T(8,128)S(1)} fusion(bf16[256,32,64]{2,1,0:T(8,128)(2,1)S(1)} %copy.26, bf16[256,64,64]{2,1,0:T(8,128)(2,1)} %copy.27), kind=kOutput, calls=%fused_computation.32 | convolution fusion | flops 67108864 | bytes 5242880 | tf_op jit(solution)/shard_map/frk,fkm->frm/dot_general | solution.py:52
  144.4 0.0 copy-done.4
  144.4 3.8 %fusion.7 = bf16[16,32,64]{2,0,1:T(8,128)(2,1)S(1)} fusion(f32[256,32,64]{2,1,0:T(8,128)S(1)} %fusion.16, s32[256]{0:T(256)S(1)} %copy-done.4), kind=kOutput, calls=%fused_computation.14 | convolution fusion | flops 100700160 | bytes 2163712 | tf_op jit(solution)/shard_map/cf,frm->crm/dot_general | solution.py:55
  148.2 4.5 %all-to-all-done = bf16[256,32,256]{2,1,0:T(8,128)(2,1)} async-done(((bf16[256,32,256]{2,1,0:T(8,128)(2,1)}), bf16[256,32,256]{2,1,0:T(8,128)(2,1)}, u32[]{:S(2)}, u32[]{:S(2)}) %all-to-all-start) | async-done | bytes 4194336 | tf_op jit(solution)/shard_map/all_to_all | solution.py:42
  152.7 3.2 %convert_reduce_fusion = f32[16,32,256]{2,1,0:T(8,128)S(1)} fusion(bf16[16,16,32,256]{3,2,1,0:T(8,128)(2,1)} %bitcast.5), kind=kLoop, calls=%fused_computation.3 | loop fusion | flops 4063232 | bytes 4718592 | tf_op jit(solution)/shard_map/reduce_sum | solution.py:43
  155.8 0.0 copy-done
  155.8 0.2 fusion.6
  156.1 0.7 copy.32
  (4 shorter events, 0.0 us)
Async XLA Ops:
  6.5 149.3 %copy-start = (bf16[16,64,256]{2,1,0:T(8,128)(2,1)S(1)}, bf16[16,64,256]{2,1,0:T(8,128)(2,1)}, u32[]{:S(2)}) copy-start(bf16[16,64,256]{2,1,0:T(8,128)(2,1)} %param.18) | copy-start | bytes 1572868
  47.0 7.1 %copy-start.2 = (bf16[32,4096]{1,0:T(8,128)(2,1)S(1)}, bf16[32,4096]{1,0:T(8,128)(2,1)}, u32[]{:S(2)}) copy-start(bf16[32,4096]{1,0:T(8,128)(2,1)} %param.11) | copy-start | bytes 786436
  47.0 7.1 %copy-start.3 = (bf16[16,64,256]{2,1,0:T(8,128)(2,1)S(1)}, bf16[16,64,256]{2,1,0:T(8,128)(2,1)}, u32[]{:S(2)}) copy-start(bf16[16,64,256]{2,1,0:T(8,128)(2,1)} %param.17) | copy-start | bytes 1572868
  47.0 8.2 %copy-start.1 = (bf16[256,64,64]{0,2,1:T(8,128)(2,1)S(1)}, bf16[256,64,64]{0,2,1:T(8,128)(2,1)}, u32[]{:S(2)}) copy-start(bf16[256,64,64]{0,2,1:T(8,128)(2,1)} %param.19) | copy-start | bytes 6291460
  47.0 105.7 %all-to-all-start = ((bf16[256,32,256]{2,1,0:T(8,128)(2,1)}), bf16[256,32,256]{2,1,0:T(8,128)(2,1)}, u32[]{:S(2)}, u32[]{:S(2)}) async-start(bf16[256,32,256]{2,1,0:T(8,128)(2,1)} %convert_element_type.23), calls=%async_computation | async-start | bytes 8388608 | tf_op jit(solution)/shard_map/all_to_all | solution.py:42
  53.9 8.1 %copy-start.5 = (s32[256]{0:T(256)S(1)}, s32[256]{0:T(256)}, u32[]{:S(2)}) copy-start(s32[256]{0:T(256)} %param.20) | copy-start | bytes 3076
  53.9 77.8 %all-gather.2.cloned.1.call-start = ((), (), s32[]{:S(2)}) async-start(), calls=%async_computation.1 | async-start | bytes 1114112 | tf_op jit(solution)/shard_map/all_gather | solution.py:50
  141.0 3.4 %copy-start.4 = (s32[256]{0:T(256)S(1)}, s32[256]{0:T(256)}, u32[]{:S(2)}) copy-start(s32[256]{0:T(256)} %param.21) | copy-start | bytes 3076
Sparse Core Ops, SparseCore 0:
  56.9 74.7 all-gather.1
where the time goes:
time: 164 us
  waiting for transfers between devices  74.2 us (45%)
  other arithmetic  28.7 us (18%)
  local copies, waits for them, and re-layouts  22.4 us (14%)
  matrix products  17.8 us (11%)
  between operations  13.5 us (8%)
  starting transfers between devices  7.1 us (4%)
    all_gather x1, waiting for transfers between devices, shards(): every = lax.all_gather(skeleton, 'wide', axis=0, tiled=True)  69.7 us
    scatter-add x1, other arithmetic, shards(): local_sums = jnp.zeros((owners * clusters_here, rhs_count, block), jnp.fl...  15.4 us
    dot_general x1, matrix products, shards(): jnp.einsum('rps,pts->prt', picked, near_blocks, preferred_element_type=jn...  10.1 us
    all_to_all x1, starting transfers between devices, shards(): lax.all_to_all(outgoing, 'wide', split_axis=0, concat_axis=0, tiled=True)  6.88 us
    unnamed x13, local copies, waits for them, and re-layouts  6.7 us
    convert_element_type x1, other arithmetic, shards(): outgoing = local_sums.astype(jnp.bfloat16)  6 us
    all_to_all x1, waiting for transfers between devices, shards(): lax.all_to_all(outgoing, 'wide', split_axis=0, concat_axis=0, tiled=True)  4.46 us
    broadcast_in_dim x1, local copies, waits for them, and re-layouts, shards(): jnp.zeros((owners * clusters_here, rhs_count, block), jnp.float32)  4.29 us
  transfers between devices with their start and end apart: 2, of which 2 were waited for; matrix products, arithmetic and copies ran while one was open for 15% of the time, Pallas kernels for 0%

commit v1 on v0

v1 whole, which is shorter than its diff:
```python
import functools

import jax
import jax.numpy as jnp
from jax import lax
from jax.experimental import pallas as pl
from jax.experimental.pallas import tpu as pltpu
from jax.sharding import PartitionSpec as P

CAP = 6
VMEM_LIMIT = 56 * 1024 * 1024
SMEM = pl.BlockSpec(memory_space=pltpu.SMEM)
VMEM = pl.BlockSpec(memory_space=pltpu.VMEM)
TRANSPOSED = (((1,), (1,)), ((), ()))
PLAIN = (((1,), (0,)), ((), ()))


def dot(a, b, dims=PLAIN):
    return lax.dot_general(a, b, dims, preferred_element_type=jnp.float32)


def prep_kernel(owners, target_ref, x_ref, basis_ref, skeleton_ref, slot_ref, code_ref, count_ref):
    clusters, rank, block = basis_ref.shape
    for o in range(owners):
        count_ref[o] = 0
    if code_ref.shape[0] != target_ref.shape[0]:
        @pl.loop(0, code_ref.shape[0])
        def _(j):
            code_ref[j] = -1

    @pl.loop(0, target_ref.shape[0])
    def _(p):
        t = target_ref[p]
        o = lax.div(t, clusters)
        c = count_ref[o]
        s = o * CAP + c
        slot_ref[p] = s
        code_ref[s] = t - o * clusters
        count_ref[o] = c + 1

    for c in range(0, clusters, 2):
        parts = [
            dot(x_ref[:, (c + i) * block:(c + i + 1) * block], basis_ref[c + i], TRANSPOSED)
            for i in range(2)
        ]
        skeleton_ref[:, c * rank:(c + 2) * rank] = jnp.concatenate(parts, axis=1).astype(
            jnp.bfloat16
        )


def near_kernel(
    pairs, slots, slot_ref, source_ref, index_ref, table_ref, x_ref, blocks_ref, out_ref
):
    step = pl.program_id(0)
    chunk, block, _ = blocks_ref.shape
    if slots != pairs:
        @pl.when(step == 0)
        def _():
            out_ref[...] = jnp.zeros_like(out_ref)

    for k in range(chunk):
        p = step * chunk + k
        xs = x_ref[:, pl.ds(pl.multiple_of(source_ref[p] * block, block), block)]
        product = dot(xs, blocks_ref[k], TRANSPOSED) * table_ref[index_ref[p]]
        out_ref[slot_ref[p]] = product.astype(jnp.bfloat16)


def far_kernel(source_ref, target_ref, skeleton_ref, couplings_ref, basis_ref, out_ref, acc_ref):
    step = pl.program_id(0)
    chunk, rank, _ = couplings_ref.shape
    clusters, _, block = basis_ref.shape
    rhs = skeleton_ref.shape[1]

    @pl.when(step == 0)
    def _():
        acc_ref[...] = jnp.zeros_like(acc_ref)

    half_of_lane = lax.broadcasted_iota(jnp.int32, (rhs, 2 * rank), 1) // rank
    group = 8
    for start in range(0, chunk, group):
        results = []
        for k in range(start, start + group):
            g = source_ref[step * chunk + k]
            owner = lax.div(g, clusters)
            inner = g - owner * clusters
            pair = lax.div(inner, 2)
            lanes = pl.ds(pl.multiple_of(pair * (2 * rank), 2 * rank), 2 * rank)
            both = skeleton_ref[owner, :, lanes]
            chosen = jnp.where(half_of_lane == inner - 2 * pair, both, jnp.zeros_like(both))
            coupling = couplings_ref[k]
            results.append(dot(chosen, jnp.concatenate([coupling, coupling], axis=0)))
        for k in range(group):
            t = target_ref[step * chunk + start + k]
            acc_ref[t] += results[k]

    @pl.when(step == pl.num_programs(0) - 1)
    def _():
        for c in range(clusters):
            out_ref[:, c * block:(c + 1) * block] = dot(
                acc_ref[c].astype(jnp.bfloat16), basis_ref[c]
            )


def final_kernel(owners, slots, code_ref, arrived_ref, far_ref, out_ref, acc_ref):
    block = arrived_ref.shape[2]
    me = lax.axis_index("wide")
    acc_ref[...] = far_ref[...]
    for d in range(owners):
        for k in range(CAP):
            c = jnp.maximum(code_ref[d * slots + me * CAP + k], 0)
            lanes = pl.ds(pl.multiple_of(c * block, block), block)
            acc_ref[:, lanes] += arrived_ref[d * CAP + k].astype(jnp.float32)
    out_ref[...] = acc_ref[...].astype(jnp.bfloat16)


def shards(
    sources,
    near_blocks,
    scale_table,
    scale_index,
    near_source,
    near_target,
    basis_in,
    basis_out,
    couplings,
    far_source,
    far_target,
):
    owners = lax.axis_size("wide")
    clusters, rank, block = basis_in.shape
    rhs = sources.shape[0]
    pairs = near_blocks.shape[0]
    fars = couplings.shape[0]
    slots = owners * CAP
    params = functools.partial(pltpu.CompilerParams, vmem_limit_bytes=VMEM_LIMIT)

    skeleton, slot, code = pl.pallas_call(
        functools.partial(prep_kernel, owners),
        out_shape=(
            jax.ShapeDtypeStruct((rhs, clusters * rank), jnp.bfloat16),
            jax.ShapeDtypeStruct((pairs,), jnp.int32),
            jax.ShapeDtypeStruct((slots,), jnp.int32),
        ),
        in_specs=[SMEM, VMEM, VMEM],
        out_specs=(VMEM, SMEM, SMEM),
        scratch_shapes=[pltpu.SMEM((owners,), jnp.int32)],
        compiler_params=params(),
        cost_estimate=pl.CostEstimate(
            flops=2 * rhs * rank * block * clusters, bytes_accessed=2 ** 20, transcendentals=0
        ),
    )(near_target, sources, basis_in)
    every = lax.all_gather(skeleton, "wide", axis=0, tiled=False)
    codes = lax.all_gather(code, "wide", axis=0, tiled=True)

    chunk = 12
    products = pl.pallas_call(
        functools.partial(near_kernel, pairs, slots),
        grid=(pairs // chunk,),
        out_shape=jax.ShapeDtypeStruct((slots, rhs, block), jnp.bfloat16),
        in_specs=[SMEM, SMEM, SMEM, SMEM, VMEM,
                  pl.BlockSpec((chunk, block, block), lambda i: (i, 0, 0))],
        out_specs=pl.BlockSpec((slots, rhs, block), lambda i: (0, 0, 0)),
        compiler_params=params(),
        cost_estimate=pl.CostEstimate(
            flops=2 * rhs * block * block * pairs,
            bytes_accessed=2 * pairs * block * block,
            transcendentals=0,
        ),
    )(slot, near_source, scale_index, scale_table, sources, near_blocks)
    arrived = lax.all_to_all(products, "wide", split_axis=0, concat_axis=0, tiled=True)

    far_chunk = 32
    far = pl.pallas_call(
        far_kernel,
        grid=(fars // far_chunk,),
        out_shape=jax.ShapeDtypeStruct((rhs, clusters * block), jnp.float32),
        in_specs=[SMEM, SMEM, VMEM,
                  pl.BlockSpec((far_chunk, rank, rank), lambda i: (i, 0, 0)), VMEM],
        out_specs=pl.BlockSpec((rhs, clusters * block), lambda i: (0, 0)),
        scratch_shapes=[pltpu.VMEM((clusters, rhs, rank), jnp.float32)],
        compiler_params=params(),
        cost_estimate=pl.CostEstimate(
            flops=2 * rhs * rank * (rank * fars + block * clusters),
            bytes_accessed=4 * fars * rank * rank + 2 ** 21,
            transcendentals=0,
        ),
    )(far_source, far_target, every, couplings, basis_out)

    return pl.pallas_call(
        functools.partial(final_kernel, owners, slots),
        out_shape=jax.ShapeDtypeStruct((rhs, clusters * block), jnp.bfloat16),
        in_specs=[SMEM, VMEM, VMEM],
        out_specs=VMEM,
        scratch_shapes=[pltpu.VMEM((rhs, clusters * block), jnp.float32)],
        compiler_params=params(),
    )(codes, arrived, far)


def solution(mesh):
    in_specs = (
        P("groups", "wide"),
        P(("groups", "wide"), None, None),
        P("groups"),
        P(("groups", "wide")),
        P(("groups", "wide")),
        P(("groups", "wide")),
        P(("groups", "wide"), None, None),
        P(("groups", "wide"), None, None),
        P(("groups", "wide"), None, None),
        P(("groups", "wide")),
        P(("groups", "wide")),
    )
    out_specs = P("groups", "wide")
    return jax.shard_map(shards, mesh=mesh, in_specs=in_specs, out_specs=out_specs, check_vma=False)
```

time: 164 us -> 96.7 us (0.59)
  the two profiles are of different devices: /device:TPU:15 before, /device:TPU:0 now
where the time goes in v1:
time: 96.7 us; the launch traced here: 96.2 us
  blocking collectives  32.6 us (34%)
  Pallas kernels  24.1 us (25%)
  between operations  14.1 us (15%)
  local copies, waits for them, and re-layouts  9.5 us (10%)
  waiting for transfers between devices  8.45 us (9%)
  starting transfers between devices  7.43 us (8%)
    unnamed x1, blocking collectives  32.6 us
    pallas_call x1, Pallas kernels, shards(): pl.pallas_call(functools.partial(near_kernel, pairs, slots), grid=(pairs...  10.1 us
    unnamed x10, local copies, waits for them, and re-layouts  9.5 us
    pallas_call x1, Pallas kernels, shards(): pl.pallas_call(far_kernel, grid=(fars // far_chunk,), out_shape=jax.Shape...  7.88 us
    all_gather x1, waiting for transfers between devices, shards(): every = lax.all_gather(skeleton, 'wide', axis=0, tiled=False)  7.77 us
    all_to_all x1, starting transfers between devices, shards(): lax.all_to_all(products, 'wide', split_axis=0, concat_axis=0, tiled=True)  7.39 us
    pallas_call x1, Pallas kernels, shards(): pl.pallas_call(functools.partial(prep_kernel, owners), out_shape=(jax.Sha...  3.17 us
    pallas_call x1, Pallas kernels, shards(): pl.pallas_call(functools.partial(final_kernel, owners, slots), out_shape=...  2.91 us
  transfers between devices with their start and end apart: 2, of which 1 were waited for; matrix products, arithmetic and copies ran while one was open for 9% of the time, Pallas kernels for 8%

profile of v1, /device:TPU:0, one launch (start us, length us, event | category | flops | bytes accessed | tf_op | source)
XLA Modules:
  0.0 96.2 jit_solution(13893564908776037252)
XLA Ops:
  6.5 3.2 %shard_map.109 = (bf16[32,1024]{1,0:T(8,128)(2,1)}, s32[96]{0:T(128)}, s32[96]{0:T(128)}) custom-call(s32[96]{0:T(128)} %target_ref.2, bf16[32,4096]{1,0:T(8,128)(2,1)} %x_ref.3, bf16[16,64,256]{2,1,0:T(8,128)(2,1)} %basis_ref.2), custom_call_target="tpu_custom_call" | custom-call | flops 16777216 | bytes 1048576 | tf_op jit(solution)/shard_map/pallas_call | solution.py:137
  9.7 10.1 %shard_map.110 = bf16[96,32,256]{2,1,0:T(8,128)(2,1)} custom-call(s32[96]{0:T(128)} %get-tuple-element.9.slot_ref, s32[96]{0:T(128)} %source_ref.2, s32[96]{0:T(128)} %index_ref.1, f32[768]{0:T(1024)} %table_ref.1, bf16[32,4096]{1,0:T(8,128)(2,1)} %x_ref.3, bf16[96,256,256]{2,1,0:T(8,128)(2,1)} %blocks_ref.1), custom_call_target="tpu_custom_call" | custom-call | flops 402653184 | bytes 12582912 | tf_op jit(solution)/shard_map/pallas_call | solution.py:156
  19.8 7.4 %all-to-all-start = ((bf16[96,32,256]{2,1,0:T(8,128)(2,1)}), bf16[96,32,256]{2,1,0:T(8,128)(2,1)S(1)}, u32[]{:S(2)}, u32[]{:S(2)}) async-start(bf16[96,32,256]{2,1,0:T(8,128)(2,1)} %shard_map.110), calls=%async_computation | async-start | bytes 3145728 | tf_op jit(solution)/shard_map/all_to_all | solution.py:170
  27.2 0.0 all-gather.3.cloned.1.call-start
  27.3 0.7 all-gather.3.cloned.1.call-update
  28.0 0.0 copy-start.2
  28.0 0.0 copy-start.1
  28.0 7.5 %copy.12.couplings_ref = bf16[256,64,64]{2,1,0:T(8,128)(2,1)} copy(bf16[256,64,64]{0,2,1:T(8,128)(2,1)} %param.19) | data formatting | bytes 4194304 | tf_op args[8]
  35.5 0.0 copy-done.2
  35.5 0.6 dynamic-slice
  36.7 0.0 copy-done.1
  36.7 0.3 dynamic-update-slice
  37.0 32.6 %all-reduce.code_ref = s32[1536]{0:T(1024)} all-reduce(s32[1536]{0:T(1024)S(1)} %dynamic-update-slice), channel_id=1, replica_groups=mesh['groups'=2,'wide'=16] {'wide'}, use_global_device_ids=true, to_apply=%add | all-reduce | flops 1536 | bytes 12288
  69.6 7.8 %all-gather.3.cloned.1.call-done = bf16[512,1024]{1,0:T(8,128)(2,1)} async-done(((bf16[32,1024]{1,0:T(8,128)(2,1)}), bf16[512,1024]{1,0:T(8,128)(2,1)}) %all-gather.3.cloned.1.call-update) | async-done | bytes 1048592 | tf_op jit(solution)/shard_map/all_gather | solution.py:152
  77.4 7.9 %shard_map.111.far_ref = f32[32,4096]{1,0:T(8,128)} custom-call(s32[256]{0:T(256)} %source_ref.3, s32[256]{0:T(256)} %target_ref.3, bf16[16,32,1024]{2,1,0:T(8,128)(2,1)} %bitcast.2, bf16[256,64,64]{2,1,0:T(8,128)(2,1)} %copy.12.couplings_ref, bf16[16,64,256]{2,1,0:T(8,128)(2,1)} %basis_ref.3), custom_call_target="tpu_custom_call" | custom-call | flops 83886080 | bytes 6291456 | tf_op jit(solution)/shard_map/pallas_call | solution.py:173
  85.3 0.0 all-to-all-done.arrived_ref
  85.3 0.0 copy-start
  85.3 1.1 %copy-done = bf16[96,32,256]{2,1,0:T(8,128)(2,1)} copy-done((bf16[96,32,256]{2,1,0:T(8,128)(2,1)}, bf16[96,32,256]{2,1,0:T(8,128)(2,1)S(1)}, u32[]{:S(2)}) %copy-start) | copy-done | bytes 1572888
  86.4 2.9 %shard_map.112 = bf16[32,4096]{1,0:T(8,128)(2,1)} custom-call(s32[1536]{0:T(1024)} %all-reduce.code_ref, bf16[96,32,256]{2,1,0:T(8,128)(2,1)} %copy-done, f32[32,4096]{1,0:T(8,128)} %shard_map.111.far_ref), custom_call_target="tpu_custom_call" | custom-call | tf_op jit(solution)/shard_map/pallas_call | solution.py:189
  (1 shorter events, 0.0 us)
Async XLA Ops:
  19.8 65.4 %all-to-all-start = ((bf16[96,32,256]{2,1,0:T(8,128)(2,1)}), bf16[96,32,256]{2,1,0:T(8,128)(2,1)S(1)}, u32[]{:S(2)}, u32[]{:S(2)}) async-start(bf16[96,32,256]{2,1,0:T(8,128)(2,1)} %shard_map.110), calls=%async_computation | async-start | bytes 3145728 | tf_op jit(solution)/shard_map/all_to_all | solution.py:170
  27.2 50.1 %all-gather.3.cloned.1.call-start = ((), (), s32[]{:S(2)}) async-start(), calls=%async_computation.1 | async-start | bytes 1114112 | tf_op jit(solution)/shard_map/all_gather | solution.py:152
  28.0 7.5 %copy-start.2 = (u32[32]{0:T(128)S(1)}, u32[32]{0:T(128)}, u32[]{:S(2)}) copy-start(u32[32]{0:T(128)} %constant.4) | copy-start | bytes 388
  28.0 8.7 %copy-start.1 = (s32[96]{0:T(128)S(1)}, s32[96]{0:T(128)}, u32[]{:S(2)}) copy-start(s32[96]{0:T(128)} %get-tuple-element.8) | copy-start | bytes 1156
  85.3 1.2 %copy-start = (bf16[96,32,256]{2,1,0:T(8,128)(2,1)}, bf16[96,32,256]{2,1,0:T(8,128)(2,1)S(1)}, u32[]{:S(2)}) copy-start(bf16[96,32,256]{2,1,0:T(8,128)(2,1)S(1)} %all-to-all-done.arrived_ref) | copy-start | bytes 4718596
Sparse Core Ops, SparseCore 0:
  30.2 47.0 all-gather.2

commit v2 on v1

--- a/solution.py
+++ b/solution.py
@@ -8,6 +8,7 @@
 from jax.sharding import PartitionSpec as P
 
 CAP = 6
+TAIL = 16
 VMEM_LIMIT = 56 * 1024 * 1024
 SMEM = pl.BlockSpec(memory_space=pltpu.SMEM)
 VMEM = pl.BlockSpec(memory_space=pltpu.VMEM)
@@ -19,14 +20,18 @@
     return lax.dot_general(a, b, dims, preferred_element_type=jnp.float32)
 
 
-def prep_kernel(owners, target_ref, x_ref, basis_ref, skeleton_ref, slot_ref, code_ref, count_ref):
+def prep_kernel(
+    owners, target_ref, index_ref, table_ref, x_ref, basis_ref,
+    skeleton_ref, by_cluster_ref, perm_ref, code_ref, factor_ref, count_ref,
+):
     clusters, rank, block = basis_ref.shape
     for o in range(owners):
         count_ref[o] = 0
     if code_ref.shape[0] != target_ref.shape[0]:
         @pl.loop(0, code_ref.shape[0])
         def _(j):
-            code_ref[j] = -1
+            code_ref[j] = 0
+            perm_ref[j] = target_ref.shape[0]
 
     @pl.loop(0, target_ref.shape[0])
     def _(p):
@@ -34,10 +39,13 @@
         o = lax.div(t, clusters)
         c = count_ref[o]
         s = o * CAP + c
-        slot_ref[p] = s
+        perm_ref[s] = p
+        factor_ref[p] = table_ref[index_ref[p]]
         code_ref[s] = t - o * clusters
         count_ref[o] = c + 1
 
+    for c in range(clusters):
+        by_cluster_ref[c] = x_ref[:, c * block:(c + 1) * block]
     for c in range(0, clusters, 2):
         parts = [
             dot(x_ref[:, (c + i) * block:(c + i + 1) * block], basis_ref[c + i], TRANSPOSED)
@@ -48,21 +56,78 @@
         )
 
 
+def flip(index, stride):
+    return index + stride * (1 - 2 * lax.rem(lax.div(index, stride), 2))
+
+
 def near_kernel(
-    pairs, slots, slot_ref, source_ref, index_ref, table_ref, x_ref, blocks_ref, out_ref
+    owners, perm_ref, code_ref, source_ref, factor_ref, skeleton_ref, x_ref, blocks_ref,
+    out_ref, every_ref, held, products, load_sem, send_sem, recv_sem,
 ):
-    step = pl.program_id(0)
-    chunk, block, _ = blocks_ref.shape
-    if slots != pairs:
-        @pl.when(step == 0)
-        def _():
-            out_ref[...] = jnp.zeros_like(out_ref)
-
-    for k in range(chunk):
-        p = step * chunk + k
-        xs = x_ref[:, pl.ds(pl.multiple_of(source_ref[p] * block, block), block)]
-        product = dot(xs, blocks_ref[k], TRANSPOSED) * table_ref[index_ref[p]]
-        out_ref[slot_ref[p]] = product.astype(jnp.bfloat16)
+    chunks = load_sem.shape[0]
+    pairs, block, _ = blocks_ref.shape
+    chunk = pairs // chunks
+    rhs = x_ref.shape[1]
+    me = lax.axis_index("wide")
+    strides = []
+    stride = owners // 2
+    while stride:
+        strides.append(stride)
+        stride //= 2
+
+    def load(c):
+        part = pl.ds(c * chunk, chunk)
+        return pltpu.make_async_copy(blocks_ref.at[part], held.at[part], load_sem.at[c])
+
+    for c in range(chunks):
+        load(c).start()
+    every_ref[me] = skeleton_ref[...]
+    products[pairs] = jnp.zeros((rhs, block), jnp.bfloat16)
+    barrier = pltpu.get_barrier_semaphore()
+    for stride in strides:
+        pl.semaphore_signal(
+            barrier, inc=1, device_id={"wide": flip(me, stride)}, device_id_type=pl.DeviceIdType.MESH
+        )
+    pl.semaphore_wait(barrier, len(strides))
+
+    have = [(0, me)]
+    for n, stride in enumerate(strides):
+        copies = []
+        for offset, owner in have:
+            copy = pltpu.make_async_remote_copy(
+                src_ref=every_ref.at[owner],
+                dst_ref=every_ref.at[owner],
+                send_sem=send_sem.at[offset + stride],
+                recv_sem=recv_sem.at[offset + stride],
+                device_id={"wide": flip(me, stride)},
+                device_id_type=pl.DeviceIdType.MESH,
+            )
+            copy.start()
+            copies.append(copy)
+
+        @pl.loop(n * chunks // len(strides), (n + 1) * chunks // len(strides))
+        def _(c):
+            load(c).wait()
+            for k in range(chunk):
+                p = c * chunk + k
+                xs = x_ref[source_ref[p]]
+                product = dot(xs, held[p], TRANSPOSED) * factor_ref[p]
+                products[p] = product.astype(jnp.bfloat16)
+
+        for copy in copies:
+            copy.wait()
+        have = have + [(offset + stride, flip(owner, stride)) for offset, owner in have]
+
+    row = lax.broadcasted_iota(jnp.int32, (TAIL, block), 0)
+
+    @pl.loop(0, owners)
+    def _(o):
+        tail = jnp.zeros((TAIL, block), jnp.float32)
+        for k in range(CAP):
+            j = o * CAP + k
+            out_ref[o, k * rhs:(k + 1) * rhs, :] = products[perm_ref[j]]
+            tail = jnp.where(row == k, code_ref[j].astype(jnp.float32), tail)
+        out_ref[o, CAP * rhs:, :] = tail.astype(jnp.bfloat16)
 
 
 def far_kernel(source_ref, target_ref, skeleton_ref, couplings_ref, basis_ref, out_ref, acc_ref):
@@ -101,15 +166,14 @@
             )
 
 
-def final_kernel(owners, slots, code_ref, arrived_ref, far_ref, out_ref, acc_ref):
-    block = arrived_ref.shape[2]
-    me = lax.axis_index("wide")
+def final_kernel(code_ref, arrived_ref, far_ref, out_ref, acc_ref):
+    owners, _, block = arrived_ref.shape
+    rhs = out_ref.shape[0]
     acc_ref[...] = far_ref[...]
     for d in range(owners):
         for k in range(CAP):
-            c = jnp.maximum(code_ref[d * slots + me * CAP + k], 0)
-            lanes = pl.ds(pl.multiple_of(c * block, block), block)
-            acc_ref[:, lanes] += arrived_ref[d * CAP + k].astype(jnp.float32)
+            lanes = pl.ds(pl.multiple_of(code_ref[d * CAP + k] * block, block), block)
+            acc_ref[:, lanes] += arrived_ref[d, k * rhs:(k + 1) * rhs, :].astype(jnp.float32)
     out_ref[...] = acc_ref[...].astype(jnp.bfloat16)
 
 
@@ -134,40 +198,49 @@
     slots = owners * CAP
     params = functools.partial(pltpu.CompilerParams, vmem_limit_bytes=VMEM_LIMIT)
 
-    skeleton, slot, code = pl.pallas_call(
+    skeleton, by_cluster, perm, code, factor = pl.pallas_call(
         functools.partial(prep_kernel, owners),
         out_shape=(
             jax.ShapeDtypeStruct((rhs, clusters * rank), jnp.bfloat16),
-            jax.ShapeDtypeStruct((pairs,), jnp.int32),
+            jax.ShapeDtypeStruct((clusters, rhs, block), jnp.bfloat16),
             jax.ShapeDtypeStruct((slots,), jnp.int32),
-        ),
-        in_specs=[SMEM, VMEM, VMEM],
-        out_specs=(VMEM, SMEM, SMEM),
+            jax.ShapeDtypeStruct((slots,), jnp.int32),
+            jax.ShapeDtypeStruct((pairs,), jnp.float32),
+        ),
+        in_specs=[SMEM, SMEM, SMEM, VMEM, VMEM],
+        out_specs=(VMEM, VMEM, SMEM, SMEM, SMEM),
         scratch_shapes=[pltpu.SMEM((owners,), jnp.int32)],
         compiler_params=params(),
         cost_estimate=pl.CostEstimate(
             flops=2 * rhs * rank * block * clusters, bytes_accessed=2 ** 20, transcendentals=0
         ),
-    )(near_target, sources, basis_in)
-    every = lax.all_gather(skeleton, "wide", axis=0, tiled=False)
-    codes = lax.all_gather(code, "wide", axis=0, tiled=True)
-
-    chunk = 12
-    products = pl.pallas_call(
-        functools.partial(near_kernel, pairs, slots),
-        grid=(pairs // chunk,),
-        out_shape=jax.ShapeDtypeStruct((slots, rhs, block), jnp.bfloat16),
-        in_specs=[SMEM, SMEM, SMEM, SMEM, VMEM,
-                  pl.BlockSpec((chunk, block, block), lambda i: (i, 0, 0))],
-        out_specs=pl.BlockSpec((slots, rhs, block), lambda i: (0, 0, 0)),
-        compiler_params=params(),
+    )(near_target, scale_index, scale_table, sources, basis_in)
+    chunks = 8
+    height = CAP * rhs + TAIL
+    outgoing, every = pl.pallas_call(
+        functools.partial(near_kernel, owners),
+        out_shape=(
+            jax.ShapeDtypeStruct((owners, height, block), jnp.bfloat16),
+            jax.ShapeDtypeStruct((owners, rhs, clusters * rank), jnp.bfloat16),
+        ),
+        in_specs=[SMEM] * 4 + [VMEM, VMEM, pl.BlockSpec(memory_space=pl.ANY)],
+        out_specs=(VMEM, VMEM),
+        scratch_shapes=[
+            pltpu.VMEM((pairs, block, block), jnp.bfloat16),
+            pltpu.VMEM((pairs + 1, rhs, block), jnp.bfloat16),
+            pltpu.SemaphoreType.DMA((chunks,)),
+            pltpu.SemaphoreType.DMA((owners,)),
+            pltpu.SemaphoreType.DMA((owners,)),
+        ],
+        compiler_params=params(collective_id=0, has_side_effects=True),
         cost_estimate=pl.CostEstimate(
             flops=2 * rhs * block * block * pairs,
             bytes_accessed=2 * pairs * block * block,
             transcendentals=0,
         ),
-    )(slot, near_source, scale_index, scale_table, sources, near_blocks)
-    arrived = lax.all_to_all(products, "wide", split_axis=0, concat_axis=0, tiled=True)
+    )(perm, code, near_source, factor, skeleton, by_cluster, near_blocks)
+    arrived = lax.all_to_all(outgoing, "wide", split_axis=0, concat_axis=0, tiled=True)
+    codes = arrived[:, CAP * rhs:CAP * rhs + CAP, 0].astype(jnp.int32).reshape(slots)
 
     far_chunk = 32
     far = pl.pallas_call(
@@ -187,7 +260,7 @@
     )(far_source, far_target, every, couplings, basis_out)
 
     return pl.pallas_call(
-        functools.partial(final_kernel, owners, slots),
+        final_kernel,
         out_shape=jax.ShapeDtypeStruct((rhs, clusters * block), jnp.bfloat16),
         in_specs=[SMEM, VMEM, VMEM],
         out_specs=VMEM,

time: 96.7 us -> 74.3 us (0.77)
  the two profiles are of different devices: /device:TPU:0 before, /device:TPU:15 now
where the time goes in v2:
time: 74.3 us; the launch traced here: 73.9 us
  Pallas kernels  35.6 us (48%)
  waiting for transfers between devices  23.7 us (32%)
  local copies, waits for them, and re-layouts  8.29 us (11%)
  starting transfers between devices  5.89 us (8%)
    all_to_all x1, waiting for transfers between devices, shards(): lax.all_to_all(outgoing, 'wide', split_axis=0, concat_axis=0, tiled=True)  23.7 us
    pallas_call x1, Pallas kernels, shards(): pl.pallas_call(functools.partial(near_kernel, owners), out_shape=(jax.Sha...  21.4 us
    pallas_call x1, Pallas kernels, shards(): pl.pallas_call(far_kernel, grid=(fars // far_chunk,), out_shape=jax.Shape...  7.87 us
    unnamed x3, local copies, waits for them, and re-layouts  7.63 us
    all_to_all x1, starting transfers between devices, shards(): lax.all_to_all(outgoing, 'wide', split_axis=0, concat_axis=0, tiled=True)  5.89 us
    pallas_call x1, Pallas kernels, shards(): pl.pallas_call(functools.partial(prep_kernel, owners), out_shape=(jax.Sha...  3.58 us
    pallas_call x1, Pallas kernels, shards(): pl.pallas_call(final_kernel, out_shape=jax.ShapeDtypeStruct((rhs, cluster...  2.79 us
  transfers between devices with their start and end apart: 1, of which 1 were waited for; matrix products, arithmetic and copies ran while one was open for 10% of the time, Pallas kernels for 11%

profile of v2, /device:TPU:15, one launch (start us, length us, event | category | flops | bytes accessed | tf_op | source)
XLA Modules:
  0.0 73.9 jit_solution(15975418258146460126)
XLA Ops:
  0.0 3.6 %shard_map.109 = (bf16[32,1024]{1,0:T(8,128)(2,1)}, bf16[16,32,256]{2,1,0:T(8,128)(2,1)}, s32[96]{0:T(128)}, s32[96]{0:T(128)}, f32[96]{0:T(128)}) custom-call(s32[96]{0:T(128)} %target_ref.2, s32[96]{0:T(128)} %index_ref.1, f32[768]{0:T(1024)} %table_ref.1, bf16[32,4096]{1,0:T(8,128)(2,1)} %x_ref.1, bf16[16,64,256]{2,1,0:T(8,128)(2,1)} %basis_ref.2), custom_call_target="tpu_custom_call" | custom-call | flops 16777216 | bytes 1048576 | tf_op jit(solution)/shard_map/pallas_call | solution.py:201
  3.6 21.4 %shard_map.110 = (bf16[16,208,256]{2,1,0:T(8,128)(2,1)}, bf16[16,32,1024]{2,1,0:T(8,128)(2,1)}) custom-call(s32[96]{0:T(128)} %get-tuple-element.12.perm_ref, s32[96]{0:T(128)} %get-tuple-element.13.code_ref, s32[96]{0:T(128)} %source_ref.2, f32[96]{0:T(128)} %get-tuple-element.14.factor_ref, bf16[32,1024]{1,0:T(8,128)(2,1)} %get-tuple-element.15.skeleton_ref, ...), custom_call_target="tpu_custom_call" | custom-call | flops 402653184 | bytes 12582912 | tf_op jit(solution)/shard_map/pallas_call | solution.py:220
  25.0 5.9 %all-to-all-start = ((bf16[16,208,256]{2,1,0:T(8,128)(2,1)}), bf16[16,208,256]{2,1,0:T(8,128)(2,1)S(1)}, u32[]{:S(2)}, u32[]{:S(2)}) async-start(bf16[16,208,256]{2,1,0:T(8,128)(2,1)} %get-tuple-element.17), calls=%async_computation | async-start | bytes 3407872 | tf_op jit(solution)/shard_map/all_to_all | solution.py:242
  30.9 7.5 %copy.13.couplings_ref = bf16[256,64,64]{2,1,0:T(8,128)(2,1)} copy(bf16[256,64,64]{0,2,1:T(8,128)(2,1)} %param.19) | data formatting | bytes 4194304 | tf_op args[8]
  38.4 7.9 %shard_map.111.far_ref = f32[32,4096]{1,0:T(8,128)} custom-call(s32[256]{0:T(256)} %source_ref.3, s32[256]{0:T(256)} %target_ref.3, bf16[16,32,1024]{2,1,0:T(8,128)(2,1)} %get-tuple-element.18.skeleton_ref, bf16[256,64,64]{2,1,0:T(8,128)(2,1)} %copy.13.couplings_ref, bf16[16,64,256]{2,1,0:T(8,128)(2,1)} %basis_ref.3), custom_call_target="tpu_custom_call" | custom-call | flops 83886080 | bytes 6291456 | tf_op jit(solution)/shard_map/pallas_call | solution.py:246
  46.2 23.7 %all-to-all-done.arrived_ref = bf16[16,208,256]{2,1,0:T(8,128)(2,1)S(1)} async-done(((bf16[16,208,256]{2,1,0:T(8,128)(2,1)}), bf16[16,208,256]{2,1,0:T(8,128)(2,1)S(1)}, u32[]{:S(2)}, u32[]{:S(2)}) %all-to-all-start) | async-done | bytes 1703968 | tf_op jit(solution)/shard_map/all_to_all | solution.py:242
  69.9 0.0 copy-start
  69.9 0.3 convert_reduce_fusion
  70.3 0.7 reshape.4.code_ref
  70.9 0.2 copy-done
  71.1 2.8 %shard_map.112 = bf16[32,4096]{1,0:T(8,128)(2,1)} custom-call(s32[96]{0:T(128)} %reshape.4.code_ref, bf16[16,208,256]{2,1,0:T(8,128)(2,1)} %copy-done, f32[32,4096]{1,0:T(8,128)} %shard_map.111.far_ref), custom_call_target="tpu_custom_call" | custom-call | tf_op jit(solution)/shard_map/pallas_call | solution.py:262
Async XLA Ops:
  25.0 44.9 %all-to-all-start = ((bf16[16,208,256]{2,1,0:T(8,128)(2,1)}), bf16[16,208,256]{2,1,0:T(8,128)(2,1)S(1)}, u32[]{:S(2)}, u32[]{:S(2)}) async-start(bf16[16,208,256]{2,1,0:T(8,128)(2,1)} %get-tuple-element.17), calls=%async_computation | async-start | bytes 3407872 | tf_op jit(solution)/shard_map/all_to_all | solution.py:242
  69.9 1.2 %copy-start = (bf16[16,208,256]{2,1,0:T(8,128)(2,1)}, bf16[16,208,256]{2,1,0:T(8,128)(2,1)S(1)}, u32[]{:S(2)}) copy-start(bf16[16,208,256]{2,1,0:T(8,128)(2,1)S(1)} %all-to-all-done.arrived_ref) | copy-start | bytes 5111812

commit v3 on v1

--- a/solution.py
+++ b/solution.py
@@ -8,6 +8,7 @@
 from jax.sharding import PartitionSpec as P
 
 CAP = 6
+TAIL = 16
 VMEM_LIMIT = 56 * 1024 * 1024
 SMEM = pl.BlockSpec(memory_space=pltpu.SMEM)
 VMEM = pl.BlockSpec(memory_space=pltpu.VMEM)
@@ -26,7 +27,7 @@
     if code_ref.shape[0] != target_ref.shape[0]:
         @pl.loop(0, code_ref.shape[0])
         def _(j):
-            code_ref[j] = -1
+            code_ref[j] = 0
 
     @pl.loop(0, target_ref.shape[0])
     def _(p):
@@ -48,21 +49,75 @@
         )
 
 
+def flip(index, stride):
+    return index + stride * (1 - 2 * lax.rem(lax.div(index, stride), 2))
+
+
+def gather_kernel(owners, skeleton_ref, after_ref, every_ref, send_sem, recv_sem):
+    me = lax.axis_index("wide")
+    strides = []
+    stride = owners // 2
+    while stride:
+        strides.append(stride)
+        stride //= 2
+    every_ref[me] = skeleton_ref[...]
+    barrier = pltpu.get_barrier_semaphore()
+    for stride in strides:
+        pl.semaphore_signal(
+            barrier, inc=1, device_id={"wide": flip(me, stride)}, device_id_type=pl.DeviceIdType.MESH
+        )
+    pl.semaphore_wait(barrier, len(strides))
+
+    def send(offset, owner, stride):
+        copy = pltpu.make_async_remote_copy(
+            src_ref=every_ref.at[owner],
+            dst_ref=every_ref.at[owner],
+            send_sem=send_sem.at[offset + stride],
+            recv_sem=recv_sem.at[offset + stride],
+            device_id={"wide": flip(me, stride)},
+            device_id_type=pl.DeviceIdType.MESH,
+        )
+        copy.start()
+        return copy
+
+    have = [(0, me)]
+    copies = [[send(0, me, stride)] for stride in strides]
+    for n, stride in enumerate(strides):
+        for offset, owner in have[1:]:
+            copies[n].append(send(offset, owner, stride))
+        for copy in copies[n]:
+            copy.wait()
+        have = have + [(offset + stride, flip(owner, stride)) for offset, owner in have]
+
+
 def near_kernel(
-    pairs, slots, slot_ref, source_ref, index_ref, table_ref, x_ref, blocks_ref, out_ref
+    pairs, slot_ref, code_ref, source_ref, index_ref, table_ref, x_ref, blocks_ref, out_ref
 ):
     step = pl.program_id(0)
     chunk, block, _ = blocks_ref.shape
-    if slots != pairs:
-        @pl.when(step == 0)
-        def _():
+    owners = out_ref.shape[0]
+    rhs = x_ref.shape[0]
+
+    @pl.when(step == 0)
+    def _():
+        if owners * CAP != pairs:
             out_ref[...] = jnp.zeros_like(out_ref)
+        row = lax.broadcasted_iota(jnp.int32, (TAIL, block), 0)
+
+        @pl.loop(0, owners)
+        def _(o):
+            tail = jnp.zeros((TAIL, block), jnp.float32)
+            for k in range(CAP):
+                tail = jnp.where(row == k, code_ref[o * CAP + k].astype(jnp.float32), tail)
+            out_ref[o, CAP * rhs:, :] = tail.astype(jnp.bfloat16)
 
     for k in range(chunk):
         p = step * chunk + k
         xs = x_ref[:, pl.ds(pl.multiple_of(source_ref[p] * block, block), block)]
         product = dot(xs, blocks_ref[k], TRANSPOSED) * table_ref[index_ref[p]]
-        out_ref[slot_ref[p]] = product.astype(jnp.bfloat16)
+        o = lax.div(slot_ref[p], CAP)
+        rows = pl.ds(pl.multiple_of((slot_ref[p] - o * CAP) * rhs, rhs), rhs)
+        out_ref[o, rows, :] = product.astype(jnp.bfloat16)
 
 
 def far_kernel(source_ref, target_ref, skeleton_ref, couplings_ref, basis_ref, out_ref, acc_ref):
@@ -101,15 +156,14 @@
             )
 
 
-def final_kernel(owners, slots, code_ref, arrived_ref, far_ref, out_ref, acc_ref):
-    block = arrived_ref.shape[2]
-    me = lax.axis_index("wide")
+def final_kernel(code_ref, arrived_ref, far_ref, out_ref, acc_ref):
+    owners, _, block = arrived_ref.shape
+    rhs = out_ref.shape[0]
     acc_ref[...] = far_ref[...]
     for d in range(owners):
         for k in range(CAP):
-            c = jnp.maximum(code_ref[d * slots + me * CAP + k], 0)
-            lanes = pl.ds(pl.multiple_of(c * block, block), block)
-            acc_ref[:, lanes] += arrived_ref[d * CAP + k].astype(jnp.float32)
+            lanes = pl.ds(pl.multiple_of(code_ref[d * CAP + k] * block, block), block)
+            acc_ref[:, lanes] += arrived_ref[d, k * rhs:(k + 1) * rhs, :].astype(jnp.float32)
     out_ref[...] = acc_ref[...].astype(jnp.bfloat16)
 
 
@@ -149,25 +203,36 @@
             flops=2 * rhs * rank * block * clusters, bytes_accessed=2 ** 20, transcendentals=0
         ),
     )(near_target, sources, basis_in)
-    every = lax.all_gather(skeleton, "wide", axis=0, tiled=False)
-    codes = lax.all_gather(code, "wide", axis=0, tiled=True)
-
     chunk = 12
-    products = pl.pallas_call(
-        functools.partial(near_kernel, pairs, slots),
+    height = CAP * rhs + TAIL
+    outgoing = pl.pallas_call(
+        functools.partial(near_kernel, pairs),
         grid=(pairs // chunk,),
-        out_shape=jax.ShapeDtypeStruct((slots, rhs, block), jnp.bfloat16),
-        in_specs=[SMEM, SMEM, SMEM, SMEM, VMEM,
+        out_shape=jax.ShapeDtypeStruct((owners, height, block), jnp.bfloat16),
+        in_specs=[SMEM, SMEM, SMEM, SMEM, SMEM, VMEM,
                   pl.BlockSpec((chunk, block, block), lambda i: (i, 0, 0))],
-        out_specs=pl.BlockSpec((slots, rhs, block), lambda i: (0, 0, 0)),
+        out_specs=pl.BlockSpec((owners, height, block), lambda i: (0, 0, 0)),
         compiler_params=params(),
         cost_estimate=pl.CostEstimate(
             flops=2 * rhs * block * block * pairs,
             bytes_accessed=2 * pairs * block * block,
             transcendentals=0,
         ),
-    )(slot, near_source, scale_index, scale_table, sources, near_blocks)
-    arrived = lax.all_to_all(products, "wide", split_axis=0, concat_axis=0, tiled=True)
+    )(slot, code, near_source, scale_index, scale_table, sources, near_blocks)
+    arrived = lax.all_to_all(outgoing, "wide", split_axis=0, concat_axis=0, tiled=True)
+    codes = arrived[:, CAP * rhs:CAP * rhs + CAP, 0].astype(jnp.int32).reshape(slots)
+    every = pl.pallas_call(
+        functools.partial(gather_kernel, owners),
+        out_shape=jax.ShapeDtypeStruct((owners, rhs, clusters * rank), jnp.bfloat16),
+        in_specs=[VMEM, pl.BlockSpec(memory_space=pl.ANY)],
+        out_specs=VMEM,
+        scratch_shapes=[
+            pltpu.SemaphoreType.DMA((owners,)),
+            pltpu.SemaphoreType.DMA((owners,)),
+        ],
+        compiler_params=params(collective_id=0, has_side_effects=True),
+        cost_estimate=pl.CostEstimate(flops=0, bytes_accessed=2 ** 25, transcendentals=0),
+    )(skeleton, outgoing)
 
     far_chunk = 32
     far = pl.pallas_call(
@@ -187,7 +252,7 @@
     )(far_source, far_target, every, couplings, basis_out)
 
     return pl.pallas_call(
-        functools.partial(final_kernel, owners, slots),
+        final_kernel,
         out_shape=jax.ShapeDtypeStruct((rhs, clusters * block), jnp.bfloat16),
         in_specs=[SMEM, VMEM, VMEM],
         out_specs=VMEM,

time: 96.7 us -> 95 us (0.982)
  Pallas kernels: 24.1 us -> 78.3 us
  blocking collectives: 32.6 us -> 0 us
  between operations: 14.1 us -> 0.04 us
  waiting for transfers between devices: 8.45 us -> 0.01 us
  local copies, waits for them, and re-layouts: 9.5 us -> 8.3 us
    pallas_call x2 -> x3, Pallas kernels: 13 us -> 67.3 us  [the longest x1 54.1 us: shards(): pl.pallas_call(functools.partial(gather_kernel, owners), out_shape=jax.Sh...]
    unnamed x1 -> x0, blocking collectives: 32.6 us -> none
    all_gather x1 -> x0, waiting for transfers between devices: 7.77 us -> none  [shards(): every = lax.all_gather(skeleton, 'wide', axis=0, tiled=False)]
    unnamed x10 -> x3, local copies, waits for them, and re-layouts: 9.5 us -> 7.56 us
  transfers between devices with their start and end apart: 2 -> 1, of which waited for: 1 -> 0; matrix products, arithmetic and copies ran while one was open for 9% -> 8% of each run, Pallas kernels for 8% -> 66%
where the time goes in v3:
time: 95 us; the launch traced here: 94.4 us
  Pallas kernels  78.3 us (82%)
  local copies, waits for them, and re-layouts  8.3 us (9%)
  starting transfers between devices  7.39 us (8%)
    pallas_call x1, Pallas kernels, shards(): pl.pallas_call(functools.partial(gather_kernel, owners), out_shape=jax.Sh...  54.1 us
    pallas_call x1, Pallas kernels, shards(): pl.pallas_call(functools.partial(near_kernel, pairs), grid=(pairs // chun...  10.4 us
    pallas_call x1, Pallas kernels, shards(): pl.pallas_call(far_kernel, grid=(fars // far_chunk,), out_shape=jax.Shape...  7.87 us
    unnamed x3, local copies, waits for them, and re-layouts  7.56 us
    all_to_all x1, starting transfers between devices, shards(): lax.all_to_all(outgoing, 'wide', split_axis=0, concat_axis=0, tiled=True)  7.39 us
    pallas_call x1, Pallas kernels, shards(): pl.pallas_call(functools.partial(prep_kernel, owners), out_shape=(jax.Sha...  3.16 us
    pallas_call x1, Pallas kernels, shards(): pl.pallas_call(final_kernel, out_shape=jax.ShapeDtypeStruct((rhs, cluster...  2.78 us
  transfers between devices with their start and end apart: 1, of which 0 were waited for; matrix products, arithmetic and copies ran while one was open for 8% of the time, Pallas kernels for 66%

profile of v3, /device:TPU:0, one launch (start us, length us, event | category | flops | bytes accessed | tf_op | source)
XLA Modules:
  0.0 94.4 jit_solution(8963497667128099576)
XLA Ops:
  0.0 3.2 %shard_map.109 = (bf16[32,1024]{1,0:T(8,128)(2,1)}, s32[96]{0:T(128)}, s32[96]{0:T(128)}) custom-call(s32[96]{0:T(128)} %target_ref.2, bf16[32,4096]{1,0:T(8,128)(2,1)} %x_ref.3, bf16[16,64,256]{2,1,0:T(8,128)(2,1)} %basis_ref.2), custom_call_target="tpu_custom_call" | custom-call | flops 16777216 | bytes 1048576 | tf_op jit(solution)/shard_map/pallas_call | solution.py:191
  3.2 10.4 %shard_map.110.after_ref = bf16[16,208,256]{2,1,0:T(8,128)(2,1)} custom-call(s32[96]{0:T(128)} %get-tuple-element.8.slot_ref, s32[96]{0:T(128)} %get-tuple-element.9.code_ref, s32[96]{0:T(128)} %source_ref.2, s32[96]{0:T(128)} %index_ref.1, f32[768]{0:T(1024)} %table_ref.1, bf16[32,4096]{1,0:T(8,128)(2,1)} %x_ref.3, bf16[96,256,256]{2,1,0:T(8,128)(2,1)} %blocks_ref.1), custom_call_target="tpu_custom_call" | custom-call | flops 402653184 | bytes 12582912 | tf_op jit(solution)/shard_map/pallas_call | solution.py:208
  13.6 7.4 %all-to-all-start = ((bf16[16,208,256]{2,1,0:T(8,128)(2,1)}), bf16[16,208,256]{2,1,0:T(8,128)(2,1)S(1)}, u32[]{:S(2)}, u32[]{:S(2)}) async-start(bf16[16,208,256]{2,1,0:T(8,128)(2,1)} %shard_map.110.after_ref), calls=%async_computation | async-start | bytes 3407872 | tf_op jit(solution)/shard_map/all_to_all | solution.py:222
  21.0 54.1 %shard_map.111.skeleton_ref = bf16[16,32,1024]{2,1,0:T(8,128)(2,1)} custom-call(bf16[32,1024]{1,0:T(8,128)(2,1)} %get-tuple-element.10.skeleton_ref, bf16[16,208,256]{2,1,0:T(8,128)(2,1)} %shard_map.110.after_ref), custom_call_target="tpu_custom_call" | custom-call | bytes 33554432 | tf_op jit(solution)/shard_map/pallas_call | solution.py:224
  75.1 7.5 %copy.13.couplings_ref = bf16[256,64,64]{2,1,0:T(8,128)(2,1)} copy(bf16[256,64,64]{0,2,1:T(8,128)(2,1)} %param.19) | data formatting | bytes 4194304 | tf_op args[8]
  82.6 7.9 %shard_map.112.far_ref = f32[32,4096]{1,0:T(8,128)} custom-call(s32[256]{0:T(256)} %source_ref.3, s32[256]{0:T(256)} %target_ref.3, bf16[16,32,1024]{2,1,0:T(8,128)(2,1)} %shard_map.111.skeleton_ref, bf16[256,64,64]{2,1,0:T(8,128)(2,1)} %copy.13.couplings_ref, bf16[16,64,256]{2,1,0:T(8,128)(2,1)} %basis_ref.3), custom_call_target="tpu_custom_call" | custom-call | flops 83886080 | bytes 6291456 | tf_op jit(solution)/shard_map/pallas_call | solution.py:238
  90.4 0.0 all-to-all-done.arrived_ref
  90.4 0.0 copy-start
  90.4 0.3 convert_reduce_fusion
  90.8 0.7 reshape.4.code_ref
  91.5 0.1 copy-done
  91.6 2.8 %shard_map.113 = bf16[32,4096]{1,0:T(8,128)(2,1)} custom-call(s32[96]{0:T(128)} %reshape.4.code_ref, bf16[16,208,256]{2,1,0:T(8,128)(2,1)} %copy-done, f32[32,4096]{1,0:T(8,128)} %shard_map.112.far_ref), custom_call_target="tpu_custom_call" | custom-call | tf_op jit(solution)/shard_map/pallas_call | solution.py:254
Async XLA Ops:
  13.6 76.9 %all-to-all-start = ((bf16[16,208,256]{2,1,0:T(8,128)(2,1)}), bf16[16,208,256]{2,1,0:T(8,128)(2,1)S(1)}, u32[]{:S(2)}, u32[]{:S(2)}) async-start(bf16[16,208,256]{2,1,0:T(8,128)(2,1)} %shard_map.110.after_ref), calls=%async_computation | async-start | bytes 3407872 | tf_op jit(solution)/shard_map/all_to_all | solution.py:222
  90.4 1.2 %copy-start = (bf16[16,208,256]{2,1,0:T(8,128)(2,1)}, bf16[16,208,256]{2,1,0:T(8,128)(2,1)S(1)}, u32[]{:S(2)}) copy-start(bf16[16,208,256]{2,1,0:T(8,128)(2,1)S(1)} %all-to-all-done.arrived_ref) | copy-start | bytes 5111812

commit v4 on v2

--- a/solution.py
+++ b/solution.py
@@ -90,20 +90,22 @@
         )
     pl.semaphore_wait(barrier, len(strides))
 
+    def send(offset, owner, stride):
+        copy = pltpu.make_async_remote_copy(
+            src_ref=every_ref.at[owner],
+            dst_ref=every_ref.at[owner],
+            send_sem=send_sem.at[offset + stride],
+            recv_sem=recv_sem.at[offset + stride],
+            device_id={"wide": flip(me, stride)},
+            device_id_type=pl.DeviceIdType.MESH,
+        )
+        copy.start()
+        return copy
+
     have = [(0, me)]
+    waiting = [[send(0, me, stride)] for stride in strides]
     for n, stride in enumerate(strides):
-        copies = []
-        for offset, owner in have:
-            copy = pltpu.make_async_remote_copy(
-                src_ref=every_ref.at[owner],
-                dst_ref=every_ref.at[owner],
-                send_sem=send_sem.at[offset + stride],
-                recv_sem=recv_sem.at[offset + stride],
-                device_id={"wide": flip(me, stride)},
-                device_id_type=pl.DeviceIdType.MESH,
-            )
-            copy.start()
-            copies.append(copy)
+        copies = waiting[n] + [send(offset, owner, stride) for offset, owner in have[1:]]
 
         @pl.loop(n * chunks // len(strides), (n + 1) * chunks // len(strides))
         def _(c):

time: 74.3 us -> 71.5 us (0.962)
  Pallas kernels: 35.6 us -> 33.5 us
    pallas_call x1, Pallas kernels: 21.4 us -> 19.3 us  [shards(): pl.pallas_call(functools.partial(near_kernel, owners), out_shape=(jax.Sha...]
  transfers between devices with their start and end apart: 1 -> 1, of which waited for: 1 -> 1; matrix products, arithmetic and copies ran while one was open for 10% -> 11% of each run, Pallas kernels for 11% -> 11%
where the time goes in v4:
time: 71.5 us; the launch traced here: 71 us
  Pallas kernels  33.5 us (47%)
  waiting for transfers between devices  23.7 us (33%)
  local copies, waits for them, and re-layouts  8.29 us (12%)
  starting transfers between devices  5.18 us (7%)
    all_to_all x1, waiting for transfers between devices, shards(): lax.all_to_all(outgoing, 'wide', split_axis=0, concat_axis=0, tiled=True)  23.7 us
    pallas_call x1, Pallas kernels, shards(): pl.pallas_call(functools.partial(near_kernel, owners), out_shape=(jax.Sha...  19.3 us
    pallas_call x1, Pallas kernels, shards(): pl.pallas_call(far_kernel, grid=(fars // far_chunk,), out_shape=jax.Shape...  7.86 us
    unnamed x3, local copies, waits for them, and re-layouts  7.63 us
    all_to_all x1, starting transfers between devices, shards(): lax.all_to_all(outgoing, 'wide', split_axis=0, concat_axis=0, tiled=True)  5.18 us
    pallas_call x1, Pallas kernels, shards(): pl.pallas_call(functools.partial(prep_kernel, owners), out_shape=(jax.Sha...  3.58 us
    pallas_call x1, Pallas kernels, shards(): pl.pallas_call(final_kernel, out_shape=jax.ShapeDtypeStruct((rhs, cluster...  2.79 us
  transfers between devices with their start and end apart: 1, of which 1 were waited for; matrix products, arithmetic and copies ran while one was open for 11% of the time, Pallas kernels for 11%

profile of v4, /device:TPU:15, one launch (start us, length us, event | category | flops | bytes accessed | tf_op | source)
XLA Modules:
  0.0 71.0 jit_solution(9732896999953634152)
XLA Ops:
  0.0 3.6 %shard_map.109 = (bf16[32,1024]{1,0:T(8,128)(2,1)}, bf16[16,32,256]{2,1,0:T(8,128)(2,1)}, s32[96]{0:T(128)}, s32[96]{0:T(128)}, f32[96]{0:T(128)}) custom-call(s32[96]{0:T(128)} %target_ref.2, s32[96]{0:T(128)} %index_ref.1, f32[768]{0:T(1024)} %table_ref.1, bf16[32,4096]{1,0:T(8,128)(2,1)} %x_ref.1, bf16[16,64,256]{2,1,0:T(8,128)(2,1)} %basis_ref.2), custom_call_target="tpu_custom_call" | custom-call | flops 16777216 | bytes 1048576 | tf_op jit(solution)/shard_map/pallas_call | solution.py:203
  3.6 19.3 %shard_map.110 = (bf16[16,208,256]{2,1,0:T(8,128)(2,1)}, bf16[16,32,1024]{2,1,0:T(8,128)(2,1)}) custom-call(s32[96]{0:T(128)} %get-tuple-element.12.perm_ref, s32[96]{0:T(128)} %get-tuple-element.13.code_ref, s32[96]{0:T(128)} %source_ref.2, f32[96]{0:T(128)} %get-tuple-element.14.factor_ref, bf16[32,1024]{1,0:T(8,128)(2,1)} %get-tuple-element.15.skeleton_ref, ...), custom_call_target="tpu_custom_call" | custom-call | flops 402653184 | bytes 12582912 | tf_op jit(solution)/shard_map/pallas_call | solution.py:222
  22.9 5.2 %all-to-all-start = ((bf16[16,208,256]{2,1,0:T(8,128)(2,1)}), bf16[16,208,256]{2,1,0:T(8,128)(2,1)S(1)}, u32[]{:S(2)}, u32[]{:S(2)}) async-start(bf16[16,208,256]{2,1,0:T(8,128)(2,1)} %get-tuple-element.17), calls=%async_computation | async-start | bytes 3407872 | tf_op jit(solution)/shard_map/all_to_all | solution.py:244
  28.1 7.5 %copy.13.couplings_ref = bf16[256,64,64]{2,1,0:T(8,128)(2,1)} copy(bf16[256,64,64]{0,2,1:T(8,128)(2,1)} %param.19) | data formatting | bytes 4194304 | tf_op args[8]
  35.5 7.9 %shard_map.111.far_ref = f32[32,4096]{1,0:T(8,128)} custom-call(s32[256]{0:T(256)} %source_ref.3, s32[256]{0:T(256)} %target_ref.3, bf16[16,32,1024]{2,1,0:T(8,128)(2,1)} %get-tuple-element.18.skeleton_ref, bf16[256,64,64]{2,1,0:T(8,128)(2,1)} %copy.13.couplings_ref, bf16[16,64,256]{2,1,0:T(8,128)(2,1)} %basis_ref.3), custom_call_target="tpu_custom_call" | custom-call | flops 83886080 | bytes 6291456 | tf_op jit(solution)/shard_map/pallas_call | solution.py:248
  43.4 23.7 %all-to-all-done.arrived_ref = bf16[16,208,256]{2,1,0:T(8,128)(2,1)S(1)} async-done(((bf16[16,208,256]{2,1,0:T(8,128)(2,1)}), bf16[16,208,256]{2,1,0:T(8,128)(2,1)S(1)}, u32[]{:S(2)}, u32[]{:S(2)}) %all-to-all-start) | async-done | bytes 1703968 | tf_op jit(solution)/shard_map/all_to_all | solution.py:244
  67.0 0.0 copy-start
  67.0 0.3 convert_reduce_fusion
  67.4 0.7 reshape.4.code_ref
  68.1 0.2 copy-done
  68.2 2.8 %shard_map.112 = bf16[32,4096]{1,0:T(8,128)(2,1)} custom-call(s32[96]{0:T(128)} %reshape.4.code_ref, bf16[16,208,256]{2,1,0:T(8,128)(2,1)} %copy-done, f32[32,4096]{1,0:T(8,128)} %shard_map.111.far_ref), custom_call_target="tpu_custom_call" | custom-call | tf_op jit(solution)/shard_map/pallas_call | solution.py:264
Async XLA Ops:
  22.9 44.2 %all-to-all-start = ((bf16[16,208,256]{2,1,0:T(8,128)(2,1)}), bf16[16,208,256]{2,1,0:T(8,128)(2,1)S(1)}, u32[]{:S(2)}, u32[]{:S(2)}) async-start(bf16[16,208,256]{2,1,0:T(8,128)(2,1)} %get-tuple-element.17), calls=%async_computation | async-start | bytes 3407872 | tf_op jit(solution)/shard_map/all_to_all | solution.py:244
  67.0 1.2 %copy-start = (bf16[16,208,256]{2,1,0:T(8,128)(2,1)}, bf16[16,208,256]{2,1,0:T(8,128)(2,1)S(1)}, u32[]{:S(2)}) copy-start(bf16[16,208,256]{2,1,0:T(8,128)(2,1)S(1)} %all-to-all-done.arrived_ref) | copy-start | bytes 5111812
